TPU v7x, 256 devices: a whole 4x4x8 slice. The times are simulated.
256 devices in a mesh: dp: 4 (over y), vocab: 64 (over x, z, core).
Axes of the slice: x: 4, y: 4, z: 8, core: 2. Of those that a mesh axis runs over, the one named last changes fastest.
Arguments:
- hidden: bfloat16 [4096, 2304], P(('dp', 'vocab')), parts along dimension 0, may hold values from -6 to 6
- norm_gain: float32 [2304], replicated, may hold values from 0.1 to 1.9
- head_weight: bfloat16 [2304, 131072], P(None, 'vocab'), may hold values from -1.875 to 1.875
Outputs:
- log_probs: bfloat16 [4096, 131072], P(('dp', 'vocab')), parts along dimension 0
There are 4 independent parts, one for each index of `dp`. A program takes and returns all parts, laid end to end along the dimension named above; an argument that names none is the same for every part. Nothing has to cross between parts.
All inputs are finite; a program needn't handle non-finite values.
Results may differ from a plain program's by a relative error of at most 0.0025.
Values may be sent and summed in bfloat16 or wider, within the bound.
A program may use at most 64 MiB of HBM per device.

v0:
```python
import jax
import jax.numpy as jnp
from jax import lax
from jax.sharding import PartitionSpec as P


def normalize(values, norm_gain):
    wide = values.astype(jnp.float32)
    power = jnp.mean(wide * wide, axis=1, keepdims=True)
    return (wide * jax.lax.rsqrt(power + 1e-06) * norm_gain[None, :]).astype(jnp.bfloat16)


def capped(normed, head_weight):
    logits = jnp.dot(normed, head_weight, preferred_element_type=jnp.float32)
    return 15.0 * jnp.tanh(logits / 30.0)


def local(hidden, norm_gain, head_weight):
    own_normed = normalize(hidden, norm_gain)
    scaled = capped(lax.all_gather(own_normed, "vocab", axis=0, tiled=True), head_weight)
    partial_total = jnp.sum(jnp.exp(scaled - 15.0), axis=1)
    total = lax.psum(partial_total, "vocab")
    labels = (scaled - 15.0 - jnp.log(total)[:, None]).astype(jnp.bfloat16)
    return lax.all_to_all(labels, "vocab", split_axis=0, concat_axis=1, tiled=True)


def solution(mesh):
    in_specs = (P(("dp", "vocab"), None), P(), P(None, "vocab"))
    out_specs = P(("dp", "vocab"), None)
    return jax.shard_map(local, mesh=mesh, in_specs=in_specs, out_specs=out_specs, check_vma=False)
```

profile of v0, /device:TPU:1, one launch (start us, length us, event | category | flops | bytes accessed | tf_op | source)
XLA Modules:
  0.0 350.0 jit_solution(8347644644189820485)
XLA Ops:
  6.5 0.0 all-gather.2.cloned.1.call-start
  6.5 1.0 fusion
  7.6 1.6 fusion.2
  9.2 0.0 all-gather.2.cloned.1.call-update
  9.2 84.6 %all-gather.2.cloned.1.call-done = bf16[1024,2304]{1,0:T(8,128)(2,1)} async-done(((bf16[16,2304]{1,0:T(8,128)(2,1)}), bf16[1024,2304]{1,0:T(8,128)(2,1)}) %all-gather.2.cloned.1.call-update) | async-done | bytes 4718608 | tf_op jit(solution)/shard_map/all_gather | solution.py:20
  93.8 16.4 %exponential_reduce_fusion = (f32[1024]{0:T(1024)S(1)}, f32[1024,2048]{1,0:T(8,128)}) fusion(bf16[1024,2304]{1,0:T(8,128)(2,1)} %all-gather.2.cloned.1.call-done, bf16[2304,2048]{1,0:T(8,128)(2,1)} %param.5), kind=kOutput, calls=%fused_computation.1 | convolution fusion | flops 9672064000 | bytes 22548480 | tf_op jit(solution)/shard_map/dot_general | solution.py:14
  110.2 123.7 %psum.7 = f32[1024]{0:T(1024)S(1)} all-reduce(f32[1024]{0:T(1024)S(1)} %get-tuple-element.5), channel_id=1, replica_groups=mesh['dp'=4,'vocab'=64] {'vocab'}, use_global_device_ids=true, to_apply=%region_2.0 | all-reduce | flops 1024 | bytes 8192 | tf_op jit(solution)/shard_map/psum | solution.py:22
  233.9 4.4 %subtract_convert_fusion = bf16[1024,2048]{1,0:T(8,128)(2,1)S(1)} fusion(f32[1024,2048]{1,0:T(8,128)} %get-tuple-element.6, f32[1024]{0:T(1024)S(1)} %log.3), kind=kLoop, calls=%fused_computation | loop fusion | flops 10485760 | bytes 12587008 | tf_op jit(solution)/shard_map/convert_element_type | solution.py:23
  238.3 102.6 %all_to_all.19 = bf16[64,16,2048]{2,1,0:T(8,128)(2,1)S(1)} all-to-all(bf16[64,16,2048]{2,1,0:T(8,128)(2,1)S(1)} %bitcast.6), channel_id=1, replica_groups=mesh['dp'=4,'vocab'=64] {'vocab'}, dimensions={0} | all-to-all | bytes 8388608 | tf_op jit(solution)/shard_map/all_to_all | solution.py:24
  340.8 2.3 copy.5
  (2 shorter events, 0.0 us)
Async XLA Ops:
  6.5 87.3 %all-gather.2.cloned.1.call-start = ((), (), s32[]{:S(2)}) async-start(), calls=%async_computation.1 | async-start | bytes 4792320 | tf_op jit(solution)/shard_map/all_gather | solution.py:20
Sparse Core Ops, SparseCore 0:
  10.1 83.6 all-gather.1
where the time goes:
time: 350 us
  blocking collectives  226 us (65%)
  waiting for transfers between devices  84.7 us (24%)
  matrix products  16.4 us (5%)
  between operations  13.4 us (4%)
  other arithmetic  7 us (2%)
    psum x1, blocking collectives, local(): total = lax.psum(partial_total, 'vocab')  124 us
    all_to_all x1, blocking collectives, local(): lax.all_to_all(labels, 'vocab', split_axis=0, concat_axis=1, tiled=True)  103 us
    all_gather x1, waiting for transfers between devices, local(): lax.all_gather(own_normed, 'vocab', axis=0, tiled=True)  84.6 us
    dot_general x1, matrix products, capped(): logits = jnp.dot(normed, head_weight, preferred_element_type=jnp.float32)  16.4 us
  transfers between devices with their start and end apart: 1, of which 1 were waited for; matrix products, arithmetic and copies ran while one was open for 0% of the time, Pallas kernels for 0%

commit v1 on v0

v1 whole, which is shorter than its diff:
```python
import functools
import math

import jax
import jax.numpy as jnp
from jax import lax
from jax.experimental import pallas as pl
from jax.experimental.pallas import tpu as pltpu
from jax.sharding import PartitionSpec as P

X, Z, C = 4, 8, 2
N = X * Z * C
ROWS = 16
CODE = 5.5
MESH = pl.DeviceIdType.MESH
TILE = 512


def depths(q):
    return (0, 4) if q == 3 else (q + 1, 7 - q)


def make_slots():
    table = []
    for q in range(4):
        for dc in range(2):
            table += [(0, dz, dc) for dz in depths(q)]
    for q in range(4):
        for dc in range(2):
            table += [(dx, dz, dc) for dx in (1, 3) for dz in depths(q)]
    for q in range(4):
        for dc in range(2):
            table += [(2, dz, dc) for dz in depths(q)]
    return table


SLOTS = make_slots()
SLOT = {place: i for i, place in enumerate(SLOTS)}
CHUNKS = [(4 * q, 4) for q in range(4)] + [(16 + 8 * q, 8) for q in range(6)]


def kernel(hidden, gain, head, coded, shift, w, g, sbuf, rbuf, acc, w_sem, out_sem, gs_sem, gr_sem, os_sem, or_sem):
    v = lax.axis_index("vocab")
    y = lax.axis_index("dp")
    x, z, c = v // (Z * C), (v // C) % Z, v % C

    def at(dx, dz, dc):
        return (y, (((x + dx) % X) * Z + (z + dz) % Z) * C + (c + dc) % C)

    barrier = pltpu.get_barrier_semaphore()

    def greet(i, carry):
        pl.semaphore_signal(barrier, inc=1, device_id=(y, (v + i) % N), device_id_type=MESH)
        return carry

    lax.fori_loop(1, N, greet, 0)
    loads = []
    for n in range(2048 // TILE):
        cols = pl.ds(n * TILE, TILE)
        loads.append(pltpu.make_async_copy(head.at[:, cols], w.at[:, cols], w_sem.at[n]))
        loads[-1].start()

    wide = hidden[...].astype(jnp.float32)
    power = jnp.mean(wide * wide, axis=1, keepdims=True)
    own = SLOT[0, 0, 0]
    g[own] = (wide * lax.rsqrt(power + 1e-06) * gain[...]).astype(jnp.bfloat16)
    acc[...] = jnp.zeros_like(acc)
    pl.semaphore_wait(barrier, N - 1)

    sends = []
    arrivals = {}

    def push(place, count, step, cols=None):
        dx, dz, dc = place
        ex, ez, ec = step
        to = SLOT[(dx - ex) % X, (dz - ez) % Z, (dc + ec) % 2]
        src, dst = g.at[pl.ds(SLOT[place], count)], g.at[pl.ds(to, count)]
        if cols is not None:
            src, dst = src.at[:, :, cols], dst.at[:, :, cols]
        k = len(sends)
        copy = pltpu.make_async_remote_copy(
            src_ref=src, dst_ref=dst, send_sem=gs_sem.at[k], recv_sem=gr_sem.at[k],
            device_id=at(ex, ez, ec), device_id_type=MESH,
        )
        copy.start()
        sends.append(copy)
        return copy

    halves = (pl.ds(0, 1152), pl.ds(1152, 1152))
    sideways = ((1, 0, 0), (3, 0, 0), (2, 0, 0))

    def spread(place, count):
        core = push(place, count, (0, 0, 1))
        rest = [push(place, count, step) for step in sideways]
        return core, rest

    down = push((0, 0, 0), 1, (0, 7, 0))
    up = push((0, 0, 0), 1, (0, 1, 0))
    core_own, side_own = spread((0, 0, 0), 1)
    x_in, core_in = {}, {}
    out_copies = []

    def compute(first, count):
        rows = count * ROWS

        def tile(n, carry):
            cols = pl.ds(pl.multiple_of(n * TILE, TILE), TILE)
            left = g[pl.ds(first, count)].reshape(rows, 2304)
            logits = jnp.dot(left, w[:, cols], preferred_element_type=jnp.float32)
            sent = jnp.exp((15.0 * CODE) * jnp.tanh(logits * (1.0 / 30.0))).astype(jnp.bfloat16)
            sbuf[pl.ds(first, count), :, cols] = sent.reshape(count, ROWS, TILE)
            return carry

        lax.fori_loop(0, 2048 // TILE, tile, 0)
        for s in range(first, first + count):
            dx, dz, dc = SLOTS[s]
            if s == own:
                continue
            to = SLOT[(-dx) % X, (-dz) % Z, dc]
            copy = pltpu.make_async_remote_copy(
                src_ref=sbuf.at[s], dst_ref=rbuf.at[to], send_sem=os_sem.at[s], recv_sem=or_sem.at[to],
                device_id=at(dx, dz, dc), device_id_type=MESH,
            )
            copy.start()
            out_copies.append(copy)

    for q in range(4):
        k = q + 1
        if q < 3:
            down.wait_recv()
            up.wait_recv()
            if k < 3:
                down = push((0, k, 0), 1, (0, 7, 0))
                up = push((0, 8 - k, 0), 1, (0, 1, 0))
            else:
                down = push((0, 3, 0), 1, (0, 7, 0), halves[0])
                up = push((0, 5, 0), 1, (0, 1, 0), halves[1])
            core_in[q], x_in[q] = spread((0, k, 0), 2)
            core_in[q].wait_recv()
        else:
            down.wait_recv()
            up.wait_recv()
            core_in[q], x_in[q] = spread((0, 4, 0), 1)
            core_own.wait_recv()
            core_in[q].wait_recv()
        if q == 0:
            for load in loads:
                load.wait()
        compute(*CHUNKS[q])

    for q in range(4):
        sources = x_in[q][:2] + (side_own[:2] if q == 3 else [])
        for copy in sources:
            copy.wait_recv()
        swap = push((1, depths(q)[0], 0), 4, (0, 0, 1))
        swap.wait_recv()
        compute(*CHUNKS[4 + q])
    for half in range(2):
        for q in (2 * half, 2 * half + 1):
            x_in[q][2].wait_recv()
            if q == 3:
                side_own[2].wait_recv()
        swaps = [push((2, depths(q)[0], 0), 2, (0, 0, 1)) for q in (2 * half, 2 * half + 1)]
        for swap in swaps:
            swap.wait_recv()
        compute(*CHUNKS[8 + half])

    log2e = 1.0 / math.log(2.0)

    def take(s):
        dx, dz, dc = SLOTS[s]
        buf = sbuf if s == own else rbuf
        column = at(dx, dz, dc)[1] * 2048
        store = pltpu.make_async_copy(
            buf.at[s], coded.at[:, pl.ds(pl.multiple_of(column, 2048), 2048)], out_sem.at[s]
        )
        store.start()
        total = acc[...]
        for n in range(0, 2048, TILE):
            part = jnp.exp(jnp.log(buf[s, :, n : n + TILE].astype(jnp.float32)) * (1.0 / CODE) - 15.0)
            for m in range(0, TILE, 128):
                total += part[:, m : m + 128]
        acc[...] = total
        return store

    stores = [take(own)]
    for s in range(N):
        if s == own:
            continue
        dx, dz, dc = SLOTS[s]
        pltpu.make_async_remote_copy(
            src_ref=sbuf.at[s], dst_ref=rbuf.at[s], send_sem=os_sem.at[s], recv_sem=or_sem.at[s],
            device_id=at(dx, dz, dc), device_id_type=MESH,
        ).wait_recv()
        stores.append(take(s))
    total = jnp.sum(acc[...], axis=1, keepdims=True)
    shift[...] = jnp.broadcast_to(15.0 + jnp.log(total), shift.shape)
    for copy in sends:
        copy.wait_send()
    for copy in out_copies:
        copy.wait_send()
    for store in stores:
        store.wait()


def local(hidden, norm_gain, head_weight):
    vmem = pl.BlockSpec(memory_space=pltpu.VMEM)
    hbm = pl.BlockSpec(memory_space=pl.ANY)
    coded, shift = pl.pallas_call(
        kernel,
        name="gather_head_exchange",
        out_shape=(
            jax.ShapeDtypeStruct((ROWS, N * 2048), jnp.bfloat16),
            jax.ShapeDtypeStruct((ROWS, 128), jnp.float32),
        ),
        in_specs=[vmem, vmem, hbm],
        out_specs=(hbm, vmem),
        scratch_shapes=[
            pltpu.VMEM((2304, 2048), jnp.bfloat16),
            pltpu.VMEM((N, ROWS, 2304), jnp.bfloat16),
            pltpu.VMEM((N, ROWS, 2048), jnp.bfloat16),
            pltpu.VMEM((N, ROWS, 2048), jnp.bfloat16),
            pltpu.VMEM((ROWS, 128), jnp.float32),
            pltpu.SemaphoreType.DMA((2048 // TILE,)),
            pltpu.SemaphoreType.DMA((N,)),
            pltpu.SemaphoreType.DMA((N,)),
            pltpu.SemaphoreType.DMA((N,)),
            pltpu.SemaphoreType.DMA((N,)),
            pltpu.SemaphoreType.DMA((N,)),
        ],
        compiler_params=pltpu.CompilerParams(
            collective_id=0, has_side_effects=True, vmem_limit_bytes=40 * 1024 * 1024
        ),
        cost_estimate=pl.CostEstimate(
            flops=2 * N * ROWS * 2304 * 2048, bytes_accessed=18 * 1024 * 1024, transcendentals=4 * N * ROWS * 2048
        ),
    )(hidden, norm_gain[None, :], head_weight)
    scaled = jnp.log(coded.astype(jnp.float32)) * (1.0 / CODE)
    return (scaled - shift[:, :1]).astype(jnp.bfloat16)


def solution(mesh):
    in_specs = (P(("dp", "vocab"), None), P(), P(None, "vocab"))
    out_specs = P(("dp", "vocab"), None)
    return jax.shard_map(local, mesh=mesh, in_specs=in_specs, out_specs=out_specs, check_vma=False)
```

time: 350 us -> 131 us (0.37)
  blocking collectives: 226 us -> 0 us
  Pallas kernels: 0 us -> 122 us
  waiting for transfers between devices: 84.7 us -> 0 us
  matrix products: 16.4 us -> 0 us
  between operations: 13.4 us -> 0.01 us
    psum x1 -> x0, blocking collectives: 124 us -> none  [local(): total = lax.psum(partial_total, 'vocab')]
    pallas_call x0 -> x1, Pallas kernels: none -> 122 us  [local(): pl.pallas_call(kernel, name='gather_head_exchange', out_shape=(jax.ShapeD...]
    all_to_all x1 -> x0, blocking collectives: 103 us -> none  [local(): lax.all_to_all(labels, 'vocab', split_axis=0, concat_axis=1, tiled=True)]
    all_gather x1 -> x0, waiting for transfers between devices: 84.6 us -> none  [local(): lax.all_gather(own_normed, 'vocab', axis=0, tiled=True)]
    dot_general x1 -> x0, matrix products: 16.4 us -> none  [capped(): logits = jnp.dot(normed, head_weight, preferred_element_type=jnp.float32)]
    unnamed x0 -> x4, local copies, waits for them, and re-layouts: none -> 4.56 us
  transfers between devices with their start and end apart: 1 -> 0, of which waited for: 1 -> 0; matrix products, arithmetic and copies ran while one was open for 0% -> 0% of each run, Pallas kernels for 0% -> 0%
where the time goes in v1:
time: 131 us
  Pallas kernels  122 us (93%)
  local copies, waits for them, and re-layouts  5.39 us (4%)
  other arithmetic  3.54 us (3%)
    pallas_call x1, Pallas kernels, local(): pl.pallas_call(kernel, name='gather_head_exchange', out_shape=(jax.ShapeD...  122 us
    unnamed x4, local copies, waits for them, and re-layouts  4.56 us
    convert_element_type x1, other arithmetic, local(): return (scaled - shift[:, :1]).astype(jnp.bfloat16)  3.54 us

profile of v1, /device:TPU:1, one launch (start us, length us, event | category | flops | bytes accessed | tf_op | source)
XLA Modules:
  0.0 130.8 jit_solution(17093974930992696171)
XLA Ops:
  0.0 0.7 broadcast_in_dim.3.gain
  0.7 0.0 copy-start
  0.7 3.7 %copy-done = bf16[2304,2048]{1,0:T(8,128)(2,1)S(1)} copy-done((bf16[2304,2048]{1,0:T(8,128)(2,1)S(1)}, bf16[2304,2048]{1,0:T(8,128)(2,1)}, u32[]{:S(2)}) %copy-start) | copy-done | bytes 9437208
  4.4 0.0 copy-start.1
  4.4 0.9 copy-done.1
  5.3 121.9 %gather_head_exchange.1 = (bf16[16,131072]{1,0:T(8,128)(2,1)S(1)}, f32[16,128]{1,0:T(8,128)S(1)}) custom-call(bf16[16,2304]{1,0:T(8,128)(2,1)S(1)} %copy-done.1, f32[1,2304]{1,0:T(1,128)S(1)} %broadcast_in_dim.3.gain, bf16[2304,2048]{1,0:T(8,128)(2,1)S(1)} %copy-done), custom_call_target="tpu_custom_call" | custom-call | flops 9663676416 | bytes 18874368 | tf_op jit(solution)/shard_map/gather_head_exchange/pallas_call | solution.py:209
  127.2 0.1 slice_reduce_fusion
  127.3 3.5 %subtract_convert_fusion = bf16[16,131072]{1,0:T(8,128)(2,1)} fusion(bf16[16,131072]{1,0:T(8,128)(2,1)S(1)} %get-tuple-element.7, f32[16]{0:T(128)S(1)} %slice_reduce_fusion), kind=kLoop, calls=%fused_computation | loop fusion | flops 8388608 | bytes 8388672 | tf_op jit(solution)/shard_map/convert_element_type | solution.py:239
Async XLA Ops:
  0.7 3.7 %copy-start = (bf16[2304,2048]{1,0:T(8,128)(2,1)S(1)}, bf16[2304,2048]{1,0:T(8,128)(2,1)}, u32[]{:S(2)}) copy-start(bf16[2304,2048]{1,0:T(8,128)(2,1)} %head.1) | copy-start | bytes 28311556
  4.4 0.9 copy-start.1

commit v2 on v0

v2 whole, which is shorter than its diff:
```python
import jax
import jax.numpy as jnp
from jax import lax
from jax.experimental import pallas as pl
from jax.experimental.pallas import tpu as pltpu
from jax.sharding import PartitionSpec as P

X, Z, C = 4, 8, 2
N = X * Z * C
ROWS = 16
D = 2304
OWN = 2048
CODE = 5.5
MESH = pl.DeviceIdType.MESH
TILE = 1024
DEPTHS = (1, 7, 2, 6, 3, 5, 0, 4)
MIXED = (1, 7, 4, 2, 6, 3, 5, 0)


def make_slots():
    table = [(0, dz, dc) for q in range(4) for dc in range(2) for dz in DEPTHS[2 * q : 2 * q + 2]]
    for dx in (1, 3, 2):
        table += [(dx, dz, dc) for dc in range(2) for dz in DEPTHS]
    return table


SLOTS = make_slots()
SLOT = {place: i for i, place in enumerate(SLOTS)}
SELF = SLOT[0, 0, 0]


def kernel(hidden, gain, head, scaled, shift, h, gn, w, g, sbuf, rbuf, acc, in_sem, w_sem, gs_sem, gr_sem, os_sem, or_sem):
    v = lax.axis_index("vocab")
    y = lax.axis_index("dp")
    x, z, c = v // (Z * C), (v // C) % Z, v % C

    def index(dx, dz, dc):
        return (((x + dx) % X) * Z + (z + dz) % Z) * C + (c + dc) % C

    def at(dx, dz, dc):
        return (y, index(dx, dz, dc))

    barrier = pltpu.get_barrier_semaphore()
    partners = ((0, 1, 0), (0, 7, 0), (1, 0, 0), (3, 0, 0), (2, 0, 0), (0, 0, 1))
    for step in partners:
        pl.semaphore_signal(barrier, inc=1, device_id=at(*step), device_id_type=MESH)

    inputs = [pltpu.make_async_copy(hidden, h, in_sem.at[0]), pltpu.make_async_copy(gain, gn, in_sem.at[1])]
    for copy in inputs:
        copy.start()
    loads = []
    for n in range(OWN // TILE):
        cols = pl.ds(n * TILE, TILE)
        loads.append(pltpu.make_async_copy(head.at[:, cols], w.at[:, cols], w_sem.at[n]))
        loads[-1].start()
    for copy in inputs:
        copy.wait()
    wide = h[...].astype(jnp.float32)
    power = jnp.mean(wide * wide, axis=1, keepdims=True)
    g[SELF] = (wide * lax.rsqrt(power + 1e-06) * gn[...].reshape(1, D)).astype(jnp.bfloat16)
    acc[...] = jnp.zeros_like(acc)
    pl.semaphore_wait(barrier, len(partners))

    sends = []

    def push(place, count, step, cols=None):
        dx, dz, dc = place
        ex, ez, ec = step
        to = SLOT[(dx - ex) % X, (dz - ez) % Z, (dc + ec) % C]
        src, dst = g.at[pl.ds(SLOT[place], count)], g.at[pl.ds(to, count)]
        if cols is not None:
            src, dst = src.at[:, :, cols], dst.at[:, :, cols]
        k = len(sends)
        copy = pltpu.make_async_remote_copy(
            src_ref=src, dst_ref=dst, send_sem=gs_sem.at[k], recv_sem=gr_sem.at[k],
            device_id=at(*step), device_id_type=MESH,
        )
        copy.start()
        sends.append(copy)
        return copy

    from_x = {1: [], 3: [], 2: []}

    def spread(place, count):
        swap = push(place, count, (0, 0, 1))
        for dx in (1, 3, 2):
            from_x[dx].append(push(place, count, ((-dx) % X, 0, 0)))
        return swap

    def multiply(first, count):
        def tile(n, carry):
            cols = pl.ds(pl.multiple_of(n * TILE, TILE), TILE)
            left = g[pl.ds(first, count)].reshape(count * ROWS, D)
            logits = jnp.dot(left, w[:, cols], preferred_element_type=jnp.float32)
            sent = jnp.exp((15.0 * CODE) * jnp.tanh(logits * (1.0 / 30.0))).astype(jnp.bfloat16)
            sbuf[pl.ds(first, count), :, cols] = sent.reshape(count, ROWS, TILE)
            return carry

        lax.fori_loop(0, OWN // TILE, tile, 0)

    def result(s, to, step):
        return pltpu.make_async_remote_copy(
            src_ref=sbuf.at[s], dst_ref=rbuf.at[to], send_sem=os_sem.at[s], recv_sem=or_sem.at[to],
            device_id=at(*step), device_id_type=MESH,
        )

    results = []

    def compute(first, count):
        multiply(first, count)
        places = SLOTS[first : first + count]
        if count == 8:
            places = [(places[0][0], dz, places[0][2]) for dz in MIXED]
        for dx, dz, dc in places:
            if (dx, dz, dc) != (0, 0, 0):
                copy = result(SLOT[dx, dz, dc], SLOT[(-dx) % X, (-dz) % Z, dc], (dx, dz, dc))
                copy.start()
                results.append(copy)

    halves = (pl.ds(0, D // 2), pl.ds(D // 2, D // 2))
    down = push((0, 0, 0), 1, (0, 7, 0))
    up = push((0, 0, 0), 1, (0, 1, 0))
    swaps = [spread((0, 0, 0), 1)]
    for k in range(1, 4):
        down.wait_recv()
        up.wait_recv()
        last = k == 3
        down = push((0, k, 0), 1, (0, 7, 0), halves[0] if last else None)
        up = push((0, 8 - k, 0), 1, (0, 1, 0), halves[1] if last else None)
        swaps.append(spread((0, k, 0), 2))
        if k == 1:
            for load in loads:
                load.wait()
            compute(0, 2)
        else:
            swaps[k - 1].wait_recv()
            compute(4 * k - 6, 4)
    down.wait_recv()
    up.wait_recv()
    swaps.append(spread((0, 4, 0), 1))
    swaps[3].wait_recv()
    compute(10, 4)
    swaps[0].wait_recv()
    swaps[4].wait_recv()
    compute(14, 2)

    cross = {}
    for dx in (1, 3, 2):
        for copy in from_x[dx]:
            copy.wait_recv()
        cross[dx] = push((dx, 1, 0), 8, (0, 0, 1))
        compute(SLOT[dx, 1, 0], 8)
        if dx == 1:
            continue
        for late in (1, 3) if dx == 3 else (2,):
            cross[late].wait_recv()
            compute(SLOT[late, 1, 1], 8)

    def take(s, buf):
        column = index(*SLOTS[s]) * OWN
        total = acc[...]
        for n in range(0, OWN, 512):
            part = jnp.log(buf[s, :, n : n + 512].astype(jnp.float32)) * (1.0 / CODE)
            scaled[:, pl.ds(pl.multiple_of(column + n, 512), 512)] = part
            terms = jnp.exp(part - 15.0)
            for m in range(0, 512, 128):
                total += terms[:, m : m + 128]
        acc[...] = total

    take(SELF, sbuf)
    for s in range(N):
        if s != SELF:
            result(s, s, SLOTS[s]).wait_recv()
            take(s, rbuf)
    total = jnp.sum(acc[...], axis=1, keepdims=True)
    shift[...] = jnp.broadcast_to(15.0 + jnp.log(total), shift.shape)
    for copy in sends + results:
        copy.wait_send()


def local(hidden, norm_gain, head_weight):
    vmem = pl.BlockSpec(memory_space=pltpu.VMEM)
    anywhere = pl.BlockSpec(memory_space=pl.ANY)
    scaled, shift = pl.pallas_call(
        kernel,
        name="gather_head_exchange",
        out_shape=(
            jax.ShapeDtypeStruct((ROWS, N * OWN), jnp.float32),
            jax.ShapeDtypeStruct((ROWS, 128), jnp.float32),
        ),
        in_specs=[anywhere, anywhere, anywhere],
        out_specs=(vmem, vmem),
        scratch_shapes=[
            pltpu.VMEM((ROWS, D), jnp.bfloat16),
            pltpu.VMEM((D,), jnp.float32),
            pltpu.VMEM((D, OWN), jnp.bfloat16),
            pltpu.VMEM((N, ROWS, D), jnp.bfloat16),
            pltpu.VMEM((N, ROWS, OWN), jnp.bfloat16),
            pltpu.VMEM((N, ROWS, OWN), jnp.bfloat16),
            pltpu.VMEM((ROWS, 128), jnp.float32),
            pltpu.SemaphoreType.DMA((2,)),
            pltpu.SemaphoreType.DMA((OWN // TILE,)),
            pltpu.SemaphoreType.DMA((N,)),
            pltpu.SemaphoreType.DMA((N,)),
            pltpu.SemaphoreType.DMA((N,)),
            pltpu.SemaphoreType.DMA((N,)),
        ],
        compiler_params=pltpu.CompilerParams(
            collective_id=0, has_side_effects=True, vmem_limit_bytes=42 * 1024 * 1024
        ),
        cost_estimate=pl.CostEstimate(
            flops=2 * N * ROWS * D * OWN, bytes_accessed=18 * 1024 * 1024, transcendentals=4 * N * ROWS * OWN
        ),
    )(hidden, norm_gain, head_weight)
    return (scaled - shift[:, :1]).astype(jnp.bfloat16)


def solution(mesh):
    in_specs = (P(("dp", "vocab"), None), P(), P(None, "vocab"))
    out_specs = P(("dp", "vocab"), None)
    return jax.shard_map(local, mesh=mesh, in_specs=in_specs, out_specs=out_specs, check_vma=False)
```

time: 350 us -> 118 us (0.34)
  blocking collectives: 226 us -> 0 us
  Pallas kernels: 0 us -> 113 us
  waiting for transfers between devices: 84.7 us -> 0 us
  matrix products: 16.4 us -> 0 us
  between operations: 13.4 us -> 0.01 us
  other arithmetic: 7 us -> 2.54 us
    psum x1 -> x0, blocking collectives: 124 us -> none  [local(): total = lax.psum(partial_total, 'vocab')]
    pallas_call x0 -> x1, Pallas kernels: none -> 113 us  [local(): pl.pallas_call(kernel, name='gather_head_exchange', out_shape=(jax.ShapeD...]
    all_to_all x1 -> x0, blocking collectives: 103 us -> none  [local(): lax.all_to_all(labels, 'vocab', split_axis=0, concat_axis=1, tiled=True)]
    all_gather x1 -> x0, waiting for transfers between devices: 84.6 us -> none  [local(): lax.all_gather(own_normed, 'vocab', axis=0, tiled=True)]
    dot_general x1 -> x0, matrix products: 16.4 us -> none  [capped(): logits = jnp.dot(normed, head_weight, preferred_element_type=jnp.float32)]
  transfers between devices with their start and end apart: 1 -> 0, of which waited for: 1 -> 0; matrix products, arithmetic and copies ran while one was open for 0% -> 0% of each run, Pallas kernels for 0% -> 0%
where the time goes in v2:
time: 118 us; the launch traced here: 117 us
  Pallas kernels  113 us (96%)
  other arithmetic  2.54 us (2%)
  local copies, waits for them, and re-layouts  1.7 us (1%)
    pallas_call x1, Pallas kernels, local(): pl.pallas_call(kernel, name='gather_head_exchange', out_shape=(jax.ShapeD...  113 us
    convert_element_type x1, other arithmetic, local(): return (scaled - shift[:, :1]).astype(jnp.bfloat16)  2.54 us

profile of v2, /device:TPU:1, one launch (start us, length us, event | category | flops | bytes accessed | tf_op | source)
XLA Modules:
  0.0 117.4 jit_solution(3376420729003726318)
XLA Ops:
  0.0 0.0 copy-start
  0.0 0.9 copy-done
  0.9 0.0 copy-start.1
  0.9 0.7 copy-done.1
  1.6 113.1 %gather_head_exchange.1 = (f32[16,131072]{1,0:T(8,128)S(1)}, f32[16,128]{1,0:T(8,128)S(1)}) custom-call(bf16[16,2304]{1,0:T(8,128)(2,1)S(1)} %copy-done, f32[2304]{0:T(1024)S(1)} %copy-done.1, bf16[2304,2048]{1,0:T(8,128)(2,1)} %head.1), custom_call_target="tpu_custom_call" | custom-call | flops 9663676416 | bytes 18874368 | tf_op jit(solution)/shard_map/gather_head_exchange/pallas_call | solution.py:184
  114.7 0.1 slice_reduce_fusion
  114.8 2.5 %subtract_convert_fusion = bf16[16,131072]{1,0:T(8,128)(2,1)} fusion(f32[16,131072]{1,0:T(8,128)S(1)} %get-tuple-element.7, f32[16]{0:T(128)S(1)} %slice_reduce_fusion), kind=kLoop, calls=%fused_computation | loop fusion | flops 4194304 | bytes 12582976 | tf_op jit(solution)/shard_map/convert_element_type | solution.py:215
Async XLA Ops:
  0.0 0.9 copy-start
  0.9 0.7 copy-start.1

commit v3 on v2

v3 whole, which is shorter than its diff:
```python
import jax
import jax.numpy as jnp
from jax import lax
from jax.experimental import pallas as pl
from jax.experimental.pallas import tpu as pltpu
from jax.sharding import PartitionSpec as P

X, Z, C = 4, 8, 2
N = X * Z * C
ROWS = 16
D = 2304
OWN = 2048
CODE = 5.5
MESH = pl.DeviceIdType.MESH
TILE = 1024
MIXED = (1, 7, 4, 2, 6, 3, 5, 0)


def near(k):
    return (k,) if k in (0, 4) else (k, Z - k)


def blocks(dxs, ks, dc):
    return [(dx, dz, dc) for k in ks for dx in dxs for dz in near(k)]


def plan():
    here, sides, far = (0,), (1, 3), (2,)
    steps = [("ring", blocks(here, (1,), 0)), ("product", blocks(here, (1,), 0))]
    steps += [("ring", blocks(here, (2,), 0)), ("product", blocks(here, (1,), 1) + blocks(here, (2,), 0))]
    steps += [("swap", blocks(sides, (0, 1), 0)), ("product", blocks(sides, (0, 1), 0))]
    steps += [("ring", blocks(here, (3,), 0)), ("product", blocks(here, (2,), 1) + blocks(here, (3,), 0))]
    steps += [("swap", blocks(sides, (2,), 0)), ("product", blocks(sides, (0, 1), 1) + blocks(sides, (2,), 0))]
    steps += [("ring", blocks(here, (4,), 0)), ("product", blocks(here, (3,), 1) + blocks(here, (0, 4), 0))]
    steps += [("swap", blocks(sides, (3,), 0)), ("product", blocks(sides, (2,), 1) + blocks(sides, (3,), 0))]
    steps += [("product", blocks(here, (0, 4), 1))]
    steps += [("swap", blocks(sides, (4,), 0)), ("product", blocks(sides, (3,), 1) + blocks(sides, (4,), 0))]
    every = (1, 2, 3, 0, 4)
    steps += [("swap", blocks(far, (0, 1, 2, 3, 4), 0)), ("product", blocks(sides, (4,), 1))]
    steps += [("last", blocks(far, (0, 1, 2, 3, 4), 0) + blocks(far, (0, 1, 2, 3, 4), 1))]
    return steps


LATE = [(0, 1), (1, 0), (2, 1), (5, 0), (6, 1), (3, 0), (4, 1), (7, 0), (0, 0), (1, 1), (2, 0), (5, 1), (6, 0), (3, 1), (4, 0), (7, 1)]
PIECES = {0: 4, 2: 2}
PLAN = plan()
SLOTS = [place for what, places in PLAN if what != "ring" and what != "swap" for place in places]
SLOT = {place: i for i, place in enumerate(SLOTS)}
SELF = SLOT[0, 0, 0]


def kernel(hidden, gain, head, scaled, shift, w, g, sbuf, rbuf, acc, w_sem, gs_sem, gr_sem, os_sem, or_sem):
    v = lax.axis_index("vocab")
    y = lax.axis_index("dp")
    x, z, c = v // (Z * C), (v // C) % Z, v % C

    def index(dx, dz, dc):
        return (((x + dx) % X) * Z + (z + dz) % Z) * C + (c + dc) % C

    def at(dx, dz, dc):
        return (y, index(dx, dz, dc))

    barrier = pltpu.get_barrier_semaphore()
    partners = ((0, 1, 0), (0, 7, 0), (1, 0, 0), (3, 0, 0), (2, 0, 0), (0, 0, 1))
    for step in partners:
        pl.semaphore_signal(barrier, inc=1, device_id=at(*step), device_id_type=MESH)

    loads = []
    for n in range(OWN // TILE):
        cols = pl.ds(n * TILE, TILE)
        loads.append(pltpu.make_async_copy(head.at[:, cols], w.at[:, cols], w_sem.at[n]))
        loads[-1].start()
    wide = hidden[...].astype(jnp.float32)
    power = jnp.mean(wide * wide, axis=1, keepdims=True)
    g[SELF] = (wide * lax.rsqrt(power + 1e-06) * gain[...].reshape(1, D)).astype(jnp.bfloat16)
    acc[...] = jnp.zeros_like(acc)
    pl.semaphore_wait(barrier, len(partners))

    sends = []

    def push(place, count, step, cols=None):
        dx, dz, dc = place
        ex, ez, ec = step
        to = SLOT[(dx - ex) % X, (dz - ez) % Z, (dc + ec) % C]
        for i in range(count):
            px, pz, pc = SLOTS[SLOT[place] + i]
            assert SLOTS[to + i] == ((px - ex) % X, (pz - ez) % Z, (pc + ec) % C)
        src, dst = g.at[pl.ds(SLOT[place], count)], g.at[pl.ds(to, count)]
        if cols is not None:
            src, dst = src.at[:, :, cols], dst.at[:, :, cols]
        k = len(sends)
        copy = pltpu.make_async_remote_copy(
            src_ref=src, dst_ref=dst, send_sem=gs_sem.at[k], recv_sem=gr_sem.at[k],
            device_id=at(*step), device_id_type=MESH,
        )
        copy.start()
        sends.append(copy)
        return copy

    coming = {}

    def spread(places):
        count = len(places)
        swap = push(places[0], count, (0, 0, 1))
        for _, dz, _ in places:
            coming[0, dz, 1] = swap
        for dx in (1, 3, 2):
            copy = push(places[0], count, ((-dx) % X, 0, 0))
            for _, dz, _ in places:
                coming[dx, dz, 0] = copy

    def await_blocks(places):
        seen = []
        for place in places:
            copy = coming.pop(place, None)
            if copy is not None and all(copy is not other for other in seen):
                copy.wait_recv()
                seen.append(copy)

    def multiply(first, count, width=TILE, after=None):
        def tile(n, carry):
            cols = pl.ds(pl.multiple_of(n * width, width), width)
            left = g[pl.ds(first, count)].reshape(count * ROWS, D)
            logits = jnp.dot(left, w[:, cols], preferred_element_type=jnp.float32)
            sent = jnp.exp((15.0 * CODE) * jnp.tanh(logits * (1.0 / 30.0))).astype(jnp.bfloat16)
            sbuf[pl.ds(first, count), :, cols] = sent.reshape(count, ROWS, width)
            if after is not None:
                after(cols)
            return carry

        lax.fori_loop(0, OWN // width, tile, 0)

    def result(s, to, step, cols=slice(None)):
        return pltpu.make_async_remote_copy(
            src_ref=sbuf.at[s, :, cols], dst_ref=rbuf.at[to, :, cols], send_sem=os_sem.at[s], recv_sem=or_sem.at[to],
            device_id=at(*step), device_id_type=MESH,
        )

    results = []

    def depth(dz):
        part = (dz + 3) // 4
        return part * (2 - part) * (2 * dz - 1) + part * (part - 1) // 2 * (2 * Z - 2 * dz)

    def product(places, last):
        first, count = SLOT[places[0]], len(places)
        pieces = PIECES.get(first, 0)
        if pieces:

            def after(cols):
                for dx, dz, dc in places:
                    result(SLOT[dx, dz, dc], SLOT[(-dx) % X, (-dz) % Z, dc], (dx, dz, dc), cols).start()

            multiply(first, count, OWN // pieces, after)
            results.extend(result(SLOT[p], SLOT[-p[0] % X, -p[1] % Z, p[2]], p) for p in places)
            return
        multiply(first, count)
        if last:
            for target, core in LATE:
                dz, dc = (target - z + Z) % Z, (core + c) % C
                copy = result(first + 8 * dc + depth(dz), first + 8 * dc + depth((Z - dz) % Z), (2, dz, dc))
                copy.start()
                results.append(copy)
            return
        for dx, dz, dc in sorted(places, key=lambda p: (p[2], MIXED.index(p[1]))) if count > 6 else places:
            if (dx, dz, dc) != (0, 0, 0):
                copy = result(SLOT[dx, dz, dc], SLOT[(-dx) % X, (-dz) % Z, dc], (dx, dz, dc))
                copy.start()
                results.append(copy)

    halves = (pl.ds(0, D // 2), pl.ds(D // 2, D // 2))
    down = push((0, 0, 0), 1, (0, 7, 0))
    up = push((0, 0, 0), 1, (0, 1, 0))
    spread([(0, 0, 0)])
    for what, places in PLAN:
        if what == "ring":
            down.wait_recv()
            up.wait_recv()
            k = places[0][1]
            if k < 4:
                down = push((0, k, 0), 1, (0, 7, 0), halves[0] if k == 3 else None)
                up = push((0, Z - k, 0), 1, (0, 1, 0), halves[1] if k == 3 else None)
            spread(places)
        elif what == "swap":
            await_blocks(places)
            copy = push(places[0], len(places), (0, 0, 1))
            for dx, dz, _ in places:
                coming[dx, dz, 1] = copy
        else:
            await_blocks(places)
            while loads:
                loads.pop().wait()
            product(places, what == "last")

    def take(s, buf):
        column = index(*SLOTS[s]) * OWN
        total = acc[...]
        for n in range(0, OWN, 512):
            part = jnp.log(buf[s, :, n : n + 512].astype(jnp.float32)) * (1.0 / CODE)
            scaled[:, pl.ds(pl.multiple_of(column + n, 512), 512)] = part
            terms = jnp.exp(part - 15.0)
            for m in range(0, 512, 128):
                total += terms[:, m : m + 128]
        acc[...] = total

    take(SELF, sbuf)
    for copy in sends:
        copy.wait_send()
    sent = 0
    for s in range(N):
        if s != SELF:
            result(s, s, SLOTS[s]).wait_recv()
            take(s, rbuf)
        if s >= 24 and sent < len(results):
            results[sent].wait_send()
            sent += 1
    total = jnp.sum(acc[...], axis=1, keepdims=True)
    shift[...] = jnp.broadcast_to(15.0 + jnp.log(total), shift.shape)
    for copy in results[sent:]:
        copy.wait_send()


FINISH = 8
WIDTH = N * OWN // FINISH


def finish(scaled, shift, out, buf, sem):
    copies = []
    for i in range(FINISH):
        cols = pl.ds(i * WIDTH, WIDTH)
        buf[:, cols] = (scaled[:, cols] - shift[:, :1]).astype(jnp.bfloat16)
        copies.append(pltpu.make_async_copy(buf.at[:, cols], out.at[:, cols], sem.at[i]))
        copies[-1].start()
    for copy in copies:
        copy.wait()


def local(hidden, norm_gain, head_weight):
    vmem = pl.BlockSpec(memory_space=pltpu.VMEM)
    anywhere = pl.BlockSpec(memory_space=pl.ANY)
    scaled, shift = pl.pallas_call(
        kernel,
        name="gather_head_exchange",
        out_shape=(
            jax.ShapeDtypeStruct((ROWS, N * OWN), jnp.float32),
            jax.ShapeDtypeStruct((ROWS, 128), jnp.float32),
        ),
        in_specs=[vmem, vmem, anywhere],
        out_specs=(vmem, vmem),
        scratch_shapes=[
            pltpu.VMEM((D, OWN), jnp.bfloat16),
            pltpu.VMEM((N, ROWS, D), jnp.bfloat16),
            pltpu.VMEM((N, ROWS, OWN), jnp.bfloat16),
            pltpu.VMEM((N, ROWS, OWN), jnp.bfloat16),
            pltpu.VMEM((ROWS, 128), jnp.float32),
            pltpu.SemaphoreType.DMA((OWN // TILE,)),
            pltpu.SemaphoreType.DMA((N,)),
            pltpu.SemaphoreType.DMA((N,)),
            pltpu.SemaphoreType.DMA((N,)),
            pltpu.SemaphoreType.DMA((N,)),
        ],
        compiler_params=pltpu.CompilerParams(
            collective_id=0, has_side_effects=True, vmem_limit_bytes=42 * 1024 * 1024
        ),
        cost_estimate=pl.CostEstimate(
            flops=2 * N * ROWS * D * OWN, bytes_accessed=18 * 1024 * 1024, transcendentals=4 * N * ROWS * OWN
        ),
    )(hidden, norm_gain, head_weight)
    return pl.pallas_call(
        finish,
        name="finish",
        out_shape=jax.ShapeDtypeStruct((ROWS, N * OWN), jnp.bfloat16),
        in_specs=[vmem, vmem],
        out_specs=anywhere,
        scratch_shapes=[pltpu.VMEM((ROWS, N * OWN), jnp.bfloat16), pltpu.SemaphoreType.DMA((FINISH,))],
        compiler_params=pltpu.CompilerParams(vmem_limit_bytes=24 * 1024 * 1024),
        cost_estimate=pl.CostEstimate(flops=2 * ROWS * N * OWN, bytes_accessed=4 * 1024 * 1024, transcendentals=0),
    )(scaled, shift)


def solution(mesh):
    in_specs = (P(("dp", "vocab"), None), P(), P(None, "vocab"))
    out_specs = P(("dp", "vocab"), None)
    return jax.shard_map(local, mesh=mesh, in_specs=in_specs, out_specs=out_specs, check_vma=False)
```

time: 118 us -> 114 us (0.966)
  the two profiles are of different devices: /device:TPU:1 before, /device:TPU:64 now
where the time goes in v3:
time: 114 us
  Pallas kernels  112 us (98%)
  local copies, waits for them, and re-layouts  1.59 us (1%)
    pallas_call x1, Pallas kernels, local(): pl.pallas_call(kernel, name='gather_head_exchange', out_shape=(jax.ShapeD...  110 us

profile of v3, /device:TPU:64, one launch (start us, length us, event | category | flops | bytes accessed | tf_op | source)
XLA Modules:
  0.0 113.9 jit_solution(12379555364820940461)
XLA Ops:
  0.0 0.0 copy-start
  0.0 0.9 copy-done
  0.9 0.0 copy-start.1
  0.9 0.7 copy-done.1
  1.6 109.9 %gather_head_exchange.1 = (f32[16,131072]{1,0:T(8,128)S(1)}, f32[16,128]{1,0:T(8,128)S(1)}) custom-call(bf16[16,2304]{1,0:T(8,128)(2,1)S(1)} %copy-done, f32[2304]{0:T(1024)S(1)} %copy-done.1, bf16[2304,2048]{1,0:T(8,128)(2,1)} %head.1), custom_call_target="tpu_custom_call" | custom-call | flops 9663676416 | bytes 18874368 | tf_op jit(solution)/shard_map/gather_head_exchange/pallas_call | solution.py:241
  111.5 2.2 %finish.1 = bf16[16,131072]{1,0:T(8,128)(2,1)} custom-call(f32[16,131072]{1,0:T(8,128)S(1)} %get-tuple-element.7.scaled, f32[16,128]{1,0:T(8,128)S(1)} %get-tuple-element.8.shift), custom_call_target="tpu_custom_call" | custom-call | flops 4194304 | bytes 4194304 | tf_op jit(solution)/shard_map/finish/pallas_call | solution.py:269
Async XLA Ops:
  0.0 0.9 copy-start
  0.9 0.7 copy-start.1

commit v4 on v3

--- a/solution.py
+++ b/solution.py
@@ -41,8 +41,8 @@
     return steps
 
 
-LATE = [(0, 1), (1, 0), (2, 1), (5, 0), (6, 1), (3, 0), (4, 1), (7, 0), (0, 0), (1, 1), (2, 0), (5, 1), (6, 0), (3, 1), (4, 0), (7, 1)]
-PIECES = {0: 4, 2: 2}
+LATE = [(0, 1), (1, 0), (3, 1), (2, 0), (5, 1), (6, 0), (4, 1), (7, 0), (0, 0), (1, 1), (3, 0), (2, 1), (5, 0), (6, 1), (4, 0), (7, 1)]
+PIECES = {0: 4, 2: 4, 6: 2}
 PLAN = plan()
 SLOTS = [place for what, places in PLAN if what != "ring" and what != "swap" for place in places]
 SLOT = {place: i for i, place in enumerate(SLOTS)}

time: 114 us -> 114 us (level)
  the two profiles are of different devices: /device:TPU:64 before, /device:TPU:65 now
where the time goes in v4:
time: 114 us
  Pallas kernels  112 us (98%)
  local copies, waits for them, and re-layouts  1.59 us (1%)
    pallas_call x1, Pallas kernels, local(): pl.pallas_call(kernel, name='gather_head_exchange', out_shape=(jax.ShapeD...  110 us

profile of v4, /device:TPU:65, one launch (start us, length us, event | category | flops | bytes accessed | tf_op | source)
XLA Modules:
  0.0 113.7 jit_solution(8577517679134748837)
XLA Ops:
  0.0 0.0 copy-start
  0.0 0.9 copy-done
  0.9 0.0 copy-start.1
  0.9 0.7 copy-done.1
  1.6 109.8 %gather_head_exchange.1 = (f32[16,131072]{1,0:T(8,128)S(1)}, f32[16,128]{1,0:T(8,128)S(1)}) custom-call(bf16[16,2304]{1,0:T(8,128)(2,1)S(1)} %copy-done, f32[2304]{0:T(1024)S(1)} %copy-done.1, bf16[2304,2048]{1,0:T(8,128)(2,1)} %head.1), custom_call_target="tpu_custom_call" | custom-call | flops 9663676416 | bytes 18874368 | tf_op jit(solution)/shard_map/gather_head_exchange/pallas_call | solution.py:241
  111.4 2.2 %finish.1 = bf16[16,131072]{1,0:T(8,128)(2,1)} custom-call(f32[16,131072]{1,0:T(8,128)S(1)} %get-tuple-element.7.scaled, f32[16,128]{1,0:T(8,128)S(1)} %get-tuple-element.8.shift), custom_call_target="tpu_custom_call" | custom-call | flops 4194304 | bytes 4194304 | tf_op jit(solution)/shard_map/finish/pallas_call | solution.py:269
Async XLA Ops:
  0.0 0.9 copy-start
  0.9 0.7 copy-start.1

commit v5 on v4

--- a/solution.py
+++ b/solution.py
@@ -104,6 +104,9 @@
         swap = push(places[0], count, (0, 0, 1))
         for _, dz, _ in places:
             coming[0, dz, 1] = swap
+
+    def sideways(places):
+        count = len(places)
         for dx in (1, 3, 2):
             copy = push(places[0], count, ((-dx) % X, 0, 0))
             for _, dz, _ in places:
@@ -172,6 +175,8 @@
     down = push((0, 0, 0), 1, (0, 7, 0))
     up = push((0, 0, 0), 1, (0, 1, 0))
     spread([(0, 0, 0)])
+    sideways([(0, 0, 0)])
+    held_back = []
     for what, places in PLAN:
         if what == "ring":
             down.wait_recv()
@@ -181,6 +186,7 @@
                 down = push((0, k, 0), 1, (0, 7, 0), halves[0] if k == 3 else None)
                 up = push((0, Z - k, 0), 1, (0, 1, 0), halves[1] if k == 3 else None)
             spread(places)
+            held_back.append(places)
         elif what == "swap":
             await_blocks(places)
             copy = push(places[0], len(places), (0, 0, 1))
@@ -191,6 +197,8 @@
             while loads:
                 loads.pop().wait()
             product(places, what == "last")
+            while held_back:
+                sideways(held_back.pop())
 
     def take(s, buf):
         column = index(*SLOTS[s]) * OWN

time: 114 us -> 114 us (level)
  the two profiles are of different devices: /device:TPU:65 before, /device:TPU:81 now
where the time goes in v5:
time: 114 us
  Pallas kernels  112 us (98%)
  local copies, waits for them, and re-layouts  1.59 us (1%)
    pallas_call x1, Pallas kernels, local(): pl.pallas_call(kernel, name='gather_head_exchange', out_shape=(jax.ShapeD...  110 us

profile of v5, /device:TPU:81, one launch (start us, length us, event | category | flops | bytes accessed | tf_op | source)
XLA Modules:
  0.0 114.0 jit_solution(192540034230971165)
XLA Ops:
  0.0 0.0 copy-start
  0.0 0.9 copy-done
  0.9 0.0 copy-start.1
  0.9 0.7 copy-done.1
  1.6 110.1 %gather_head_exchange.1 = (f32[16,131072]{1,0:T(8,128)S(1)}, f32[16,128]{1,0:T(8,128)S(1)}) custom-call(bf16[16,2304]{1,0:T(8,128)(2,1)S(1)} %copy-done, f32[2304]{0:T(1024)S(1)} %copy-done.1, bf16[2304,2048]{1,0:T(8,128)(2,1)} %head.1), custom_call_target="tpu_custom_call" | custom-call | flops 9663676416 | bytes 18874368 | tf_op jit(solution)/shard_map/gather_head_exchange/pallas_call | solution.py:249
  111.7 2.2 %finish.1 = bf16[16,131072]{1,0:T(8,128)(2,1)} custom-call(f32[16,131072]{1,0:T(8,128)S(1)} %get-tuple-element.7.scaled, f32[16,128]{1,0:T(8,128)S(1)} %get-tuple-element.8.shift), custom_call_target="tpu_custom_call" | custom-call | flops 4194304 | bytes 4194304 | tf_op jit(solution)/shard_map/finish/pallas_call | solution.py:277
Async XLA Ops:
  0.0 0.9 copy-start
  0.9 0.7 copy-start.1
